TPU v7x, 256 devices: a whole 4x4x8 slice. The times are simulated.
256 devices in a mesh: ctx: 32 (over z_lo, y, core), wsh: 8 (over z_hi, x).
Axes of the slice: x: 4, y: 4, z: 8 (z_hi: 2, z_lo: 4; z = z_hi * 4 + z_lo), core: 2. Of those that a mesh axis runs over, the one named last changes fastest.
Arguments:
- tokens: bfloat16 [8, 16384, 768], P('wsh', 'ctx'), may hold values from -6 to 6
- teacher: bfloat16 [8, 16384, 768], P('wsh', 'ctx'), may hold values from -6 to 6
- clusters: int32 [8, 12, 16384], P('wsh', None, 'ctx'), may hold values from 0 to 127, as said below
- segments: int32 [8, 16384], P('wsh', 'ctx'), may hold values from 0 to 23, never falling along the last dimension, each value on 1 to 2000 neighbouring positions
- counted: int32 [8, 16384], P('wsh', 'ctx'), may hold values from 0 to 1, as said below
- w_qkv: bfloat16 [768, 2304], P('wsh'), may hold values from -0.21875 to 0.21875
- w_out: bfloat16 [768, 768], P('wsh'), may hold values from -0.4375 to 0.4375
- w_up: bfloat16 [768, 3072], P('wsh'), may hold values from -0.21875 to 0.21875
- w_down: bfloat16 [3072, 768], P('wsh'), may hold values from -0.109375 to 0.109375
- norms: bfloat16 [4, 768], P(None, 'wsh'), may hold values from -0.45 to 1.45
Outputs:
- activations: bfloat16 [8, 16384, 768], P('wsh', 'ctx')
- input_grad: float32 [8, 16384, 768], P('wsh', 'ctx')
- loss: float32 [], replicated
- grad_w_qkv: float32 [768, 2304], P('wsh', 'ctx')
- grad_w_out: float32 [768, 768], P('wsh', 'ctx')
- grad_w_up: float32 [768, 3072], P('wsh', 'ctx')
- grad_w_down: float32 [3072, 768], P('wsh', 'ctx')
- grad_norms: float32 [4, 768], P(None, ('ctx', 'wsh'))
Inputs may be any that keep to these rules, and one draw needn't show every extreme that they name: `clusters`: for each sequence and head every cluster number is held by exactly 128 tokens, and each aligned block of 512 positions gives exactly 16 tokens to each aligned group of 4 consecutive cluster numbers. `segments`: document numbers never fall along a sequence; a document holds 1 to 2000 tokens. `counted`: 1 on a prefix of each sequence and 0 after it; the prefix covers at least half and at most seven eighths of the sequence.
All inputs are finite; a program needn't handle non-finite values.
Results may differ from a plain program's by a relative error of at most 0.02.
Values may be sent and summed in bfloat16 or wider, within the bound.
A program may use at most 128 MiB of HBM per device.

v0:
```python
import jax
import jax.numpy as jnp
from jax import lax
from jax.sharding import PartitionSpec as P

CLUSTER = 128


def layer_norm(values, gain_row, shift_row):
    row_mean = jnp.mean(values, axis=-1, keepdims=True)
    centered = values - row_mean
    inv_scale = lax.rsqrt(jnp.mean(centered * centered, axis=-1, keepdims=True) + 1e-05)
    normed = centered * inv_scale
    return (normed * gain_row + shift_row, normed, inv_scale)


def norm_back(grad_rows, normed, inv_scale, gain_row):
    weighted = grad_rows * gain_row
    grad_input = inv_scale * (
        weighted
        - jnp.mean(weighted, axis=-1, keepdims=True)
        - normed * jnp.mean(weighted * normed, axis=-1, keepdims=True)
    )
    return (grad_input, jnp.sum(grad_rows * normed, axis=0), jnp.sum(grad_rows, axis=0))


def gelu_exact(values):
    return jax.nn.gelu(values, approximate=False)


def selector(index):
    slot_count = index.shape[1]
    source_iota = jnp.arange(slot_count, dtype=jnp.int32)[None, :, None]
    return (index[:, None, :] == source_iota).astype(jnp.bfloat16)


def permute(array, table):
    return jnp.einsum("hct,hts->hcs", array, table, preferred_element_type=jnp.float32).astype(
        jnp.bfloat16
    )


def take_index(array, index):
    return jnp.take_along_axis(array, index[:, None, :], axis=2)


def cluster_order(labels):
    slot_count = labels.shape[2]
    keys = labels[:, 0, :] * slot_count + jnp.arange(slot_count, dtype=jnp.int32)[None, :]
    order = jnp.argsort(keys, axis=1)
    inverse = jnp.argsort(order, axis=1)
    return (order, inverse)


def as_blocks(array):
    return array.reshape(array.shape[0], array.shape[1], array.shape[2] // CLUSTER, CLUSTER)


def from_blocks(array):
    return array.reshape(array.shape[0], array.shape[1], array.shape[2] * array.shape[3])


def cluster_scores(blocks, seg_blocks, head_size):
    query_rows = blocks[:, :head_size]
    key_rows = blocks[:, head_size : 2 * head_size]
    raw_scores = jnp.einsum(
        "hdgq,hdgk->hgqk", query_rows, key_rows, preferred_element_type=jnp.float32
    ) * head_size ** (-0.5)
    allowed = seg_blocks[:, :, :, None] == seg_blocks[:, :, None, :]
    return (raw_scores, allowed)


def attend_forward(blocks, seg_blocks, head_size):
    raw_scores, allowed = cluster_scores(blocks, seg_blocks, head_size)
    masked = jnp.where(allowed, raw_scores, -1e30)
    row_top = jnp.max(masked, axis=-1, keepdims=True)
    row_total = jnp.sum(jnp.where(allowed, jnp.exp(masked - row_top), 0.0), axis=-1, keepdims=True)
    logsum = row_top + jnp.log(row_total)
    weights = jnp.where(allowed, jnp.exp(raw_scores - logsum), 0.0)
    value_rows = blocks[:, 2 * head_size :]
    attended = jnp.einsum(
        "hgqk,hdgk->hdgq",
        weights.astype(jnp.bfloat16),
        value_rows,
        preferred_element_type=jnp.float32,
    )
    return (attended.astype(jnp.bfloat16), logsum)


def attend_backward(blocks, seg_blocks, logsum, grad_heads, head_size):
    raw_scores, allowed = cluster_scores(blocks, seg_blocks, head_size)
    weights = jnp.where(allowed, jnp.exp(raw_scores - logsum), 0.0)
    query_rows = blocks[:, :head_size]
    key_rows = blocks[:, head_size : 2 * head_size]
    value_rows = blocks[:, 2 * head_size :]
    grad_weights = jnp.einsum(
        "hdgq,hdgk->hgqk", grad_heads, value_rows, preferred_element_type=jnp.float32
    )
    row_delta = jnp.sum(weights * grad_weights, axis=-1, keepdims=True)
    grad_raw = (weights * (grad_weights - row_delta)).astype(jnp.bfloat16)
    factor = head_size ** (-0.5)
    grad_query = (
        jnp.einsum("hgqk,hdgk->hdgq", grad_raw, key_rows, preferred_element_type=jnp.float32)
        * factor
    )
    grad_keys = (
        jnp.einsum("hgqk,hdgq->hdgk", grad_raw, query_rows, preferred_element_type=jnp.float32)
        * factor
    )
    grad_values = jnp.einsum(
        "hgqk,hdgq->hdgk",
        weights.astype(jnp.bfloat16),
        grad_heads,
        preferred_element_type=jnp.float32,
    )
    return jnp.concatenate([grad_query, grad_keys, grad_values], axis=1).astype(jnp.bfloat16)


def local(tokens, teacher, clusters, segments, counted, w_qkv, w_out, w_up, w_down, norms):
    full_qkv, full_out, full_up, full_down, full_norms = (
        lax.all_gather(w_qkv, "wsh", axis=0, tiled=True),
        lax.all_gather(w_out, "wsh", axis=0, tiled=True),
        lax.all_gather(w_up, "wsh", axis=0, tiled=True),
        lax.all_gather(w_down, "wsh", axis=0, tiled=True),
        lax.all_gather(norms, "wsh", axis=1, tiled=True),
    )
    x_rows = tokens[0]
    tok_count, model_dim = x_rows.shape
    head_count = clusters.shape[1]
    head_size = model_dim // head_count
    peer_count = lax.axis_size("ctx")
    share_size = tok_count // peer_count
    per_device = tok_count // CLUSTER
    cluster_ids = clusters[0]
    target_dev = cluster_ids // per_device
    onehot = (target_dev[:, :, None] == jnp.arange(peer_count, dtype=jnp.int32)).astype(jnp.int32)
    within = jnp.sum((jnp.cumsum(onehot, axis=1) - 1) * onehot, axis=2)
    slot_index = target_dev * share_size + within
    head_iota = jnp.arange(head_count, dtype=jnp.int32)[:, None]
    token_iota = jnp.broadcast_to(jnp.arange(tok_count, dtype=jnp.int32)[None, :], slot_index.shape)
    send_order = jnp.zeros_like(slot_index).at[head_iota, slot_index].set(token_iota)
    send_table = selector(send_order)
    home_table = selector(slot_index)
    qkv = jnp.dot(x_rows, full_qkv, preferred_element_type=jnp.float32).astype(jnp.bfloat16)
    packed = (
        qkv.reshape(tok_count, 3, head_count, head_size)
        .transpose(2, 1, 3, 0)
        .reshape(head_count, 3 * head_size, tok_count)
    )
    seg_ids = jnp.broadcast_to(segments[0][None, :], cluster_ids.shape)
    label_pair = jnp.stack([cluster_ids, seg_ids], axis=1)
    sent_qkv = permute(packed, send_table)
    sent_labels = take_index(label_pair, send_order)
    got_qkv, got_labels = (
        lax.all_to_all(sent_qkv, "ctx", split_axis=2, concat_axis=2, tiled=True),
        lax.all_to_all(sent_labels, "ctx", split_axis=2, concat_axis=2, tiled=True),
    )
    order, inverse = cluster_order(got_labels)
    order_table = selector(order)
    inverse_table = selector(inverse)
    qkv_blocks = as_blocks(permute(got_qkv, order_table))
    seg_blocks = as_blocks(take_index(got_labels[:, 1:2, :], order))[:, 0]
    attended, logsum = attend_forward(qkv_blocks, seg_blocks, head_size)
    returned = lax.all_to_all(
        permute(from_blocks(attended), inverse_table),
        "ctx",
        split_axis=2,
        concat_axis=2,
        tiled=True,
    )
    mixed_heads = permute(returned, home_table).transpose(2, 0, 1).reshape(tok_count, model_dim)
    gain_rows = full_norms.astype(jnp.float32)
    first_sum = x_rows.astype(jnp.float32) + jnp.dot(
        mixed_heads, full_out, preferred_element_type=jnp.float32
    )
    normed_one, unit_one, scale_one = layer_norm(first_sum, gain_rows[0], gain_rows[1])
    normed_low = normed_one.astype(jnp.bfloat16)
    upper_rows = jnp.dot(normed_low, full_up, preferred_element_type=jnp.float32)
    active, gelu_back = jax.vjp(gelu_exact, upper_rows)
    active_low = active.astype(jnp.bfloat16)
    second = normed_one + jnp.dot(active_low, full_down, preferred_element_type=jnp.float32)
    result, unit_two, scale_two = layer_norm(second, gain_rows[2], gain_rows[3])
    errors = result - teacher[0].astype(jnp.float32)
    mask_rows = counted[0].astype(jnp.float32)
    partial_value = jnp.sum(mask_rows * jnp.mean(errors * errors, axis=1))
    total_error, total_count = lax.psum((partial_value, jnp.sum(mask_rows)), ("ctx", "wsh"))
    loss_value = total_error / total_count
    everyone = tok_count * peer_count * lax.axis_size("wsh")
    grad_result = everyone / total_count * mask_rows[:, None] * errors
    grad_second, grad_gain_two, grad_shift_two = norm_back(
        grad_result, unit_two, scale_two, gain_rows[2]
    )
    grad_branch_two = grad_second.astype(jnp.bfloat16)
    grad_down = jnp.dot(active_low.T, grad_branch_two, preferred_element_type=jnp.float32)
    grad_active = jnp.dot(grad_branch_two, full_down.T, preferred_element_type=jnp.float32)
    (grad_upper,) = gelu_back(grad_active)
    grad_upper_low = grad_upper.astype(jnp.bfloat16)
    grad_up = jnp.dot(normed_low.T, grad_upper_low, preferred_element_type=jnp.float32)
    grad_normed = (
        jnp.dot(grad_upper_low, full_up.T, preferred_element_type=jnp.float32) + grad_second
    )
    grad_first, grad_gain_one, grad_shift_one = norm_back(
        grad_normed, unit_one, scale_one, gain_rows[0]
    )
    grad_branch = grad_first.astype(jnp.bfloat16)
    grad_outw = jnp.dot(mixed_heads.T, grad_branch, preferred_element_type=jnp.float32)
    grad_mixed = jnp.dot(grad_branch, full_out.T, preferred_element_type=jnp.float32).astype(
        jnp.bfloat16
    )
    grad_heads = permute(
        grad_mixed.reshape(tok_count, head_count, head_size).transpose(1, 2, 0), send_table
    )
    grad_got, again_qkv, again_labels = (
        lax.all_to_all(grad_heads, "ctx", split_axis=2, concat_axis=2, tiled=True),
        lax.all_to_all(sent_qkv, "ctx", split_axis=2, concat_axis=2, tiled=True),
        lax.all_to_all(sent_labels, "ctx", split_axis=2, concat_axis=2, tiled=True),
    )
    back_order, back_inverse = cluster_order(again_labels)
    back_table = selector(back_order)
    back_home = selector(back_inverse)
    back_blocks = as_blocks(permute(again_qkv, back_table))
    back_segs = as_blocks(take_index(again_labels[:, 1:2, :], back_order))[:, 0]
    grad_blocks = as_blocks(permute(grad_got, back_table))
    grad_packed = attend_backward(back_blocks, back_segs, logsum, grad_blocks, head_size)
    grad_home = lax.all_to_all(
        permute(from_blocks(grad_packed), back_home), "ctx", split_axis=2, concat_axis=2, tiled=True
    )
    grad_qkv = (
        permute(grad_home, home_table)
        .reshape(head_count, 3, head_size, tok_count)
        .transpose(3, 1, 0, 2)
        .reshape(tok_count, 3 * model_dim)
    )
    grad_inw = jnp.dot(x_rows.T, grad_qkv, preferred_element_type=jnp.float32)
    grad_tokens = jnp.dot(grad_qkv, full_qkv.T, preferred_element_type=jnp.float32) + grad_first
    grad_norms = jnp.stack([grad_gain_one, grad_shift_one, grad_gain_two, grad_shift_two])
    part_qkv, part_out, part_up, part_down, part_norms = (
        lax.psum_scatter(
            grad_inw.astype(jnp.bfloat16), "ctx", scatter_dimension=1, tiled=True
        ).astype(jnp.float32),
        lax.psum_scatter(
            grad_outw.astype(jnp.bfloat16), "ctx", scatter_dimension=1, tiled=True
        ).astype(jnp.float32),
        lax.psum_scatter(
            grad_up.astype(jnp.bfloat16), "ctx", scatter_dimension=1, tiled=True
        ).astype(jnp.float32),
        lax.psum_scatter(
            grad_down.astype(jnp.bfloat16), "ctx", scatter_dimension=1, tiled=True
        ).astype(jnp.float32),
        lax.psum_scatter(
            grad_norms.astype(jnp.bfloat16), "ctx", scatter_dimension=1, tiled=True
        ).astype(jnp.float32),
    )
    final_qkv, final_out, final_up, final_down, final_norms = (
        lax.psum_scatter(
            part_qkv.astype(jnp.bfloat16), "wsh", scatter_dimension=0, tiled=True
        ).astype(jnp.float32),
        lax.psum_scatter(
            part_out.astype(jnp.bfloat16), "wsh", scatter_dimension=0, tiled=True
        ).astype(jnp.float32),
        lax.psum_scatter(
            part_up.astype(jnp.bfloat16), "wsh", scatter_dimension=0, tiled=True
        ).astype(jnp.float32),
        lax.psum_scatter(
            part_down.astype(jnp.bfloat16), "wsh", scatter_dimension=0, tiled=True
        ).astype(jnp.float32),
        lax.psum_scatter(
            part_norms.astype(jnp.bfloat16), "wsh", scatter_dimension=1, tiled=True
        ).astype(jnp.float32),
    )
    return (
        result.astype(jnp.bfloat16)[None],
        grad_tokens[None],
        loss_value,
        final_qkv,
        final_out,
        final_up,
        final_down,
        final_norms,
    )


def solution(mesh):
    placed = (
        P("wsh", "ctx", None),
        P("wsh", "ctx", None),
        P("wsh", None, "ctx"),
        P("wsh", "ctx"),
        P("wsh", "ctx"),
        P("wsh", None),
        P("wsh", None),
        P("wsh", None),
        P("wsh", None),
        P(None, "wsh"),
    )
    return jax.shard_map(
        local,
        mesh=mesh,
        in_specs=placed,
        out_specs=(
            P("wsh", "ctx", None),
            P("wsh", "ctx", None),
            P(),
            P("wsh", "ctx"),
            P("wsh", "ctx"),
            P("wsh", "ctx"),
            P("wsh", "ctx"),
            P(None, ("ctx", "wsh")),
        ),
        check_vma=False,
    )
```

profile of v0, /device:TPU:1, one launch (start us, length us, event | category | flops | bytes accessed | tf_op | source)
XLA Modules:
  0.0 1616.1 jit_solution(12117425152380581534)
XLA Ops:
  9.8 13.8 reduce-window.6
  25.6 23.0 %scatter_custom_fusion = s32[6144]{0:T(1024)S(1)} fusion(s32[6144]{0:T(1024)S(1)} %reshape.343, s32[6144]{0:T(1024)S(1)} %reshape.345, s32[]{:T(128)} %constant.54.clone.1), kind=kCustom, calls=%fused_computation.176 | custom fusion | bytes 24580
  50.1 66.4 %gather_fusion = s32[6144,2]{1,0:T(8,128)} fusion(s32[12,2,512]{1,2,0:T(8,128)S(1)} %copy.91, s32[6144]{0:T(1024)S(1)} %bitcast.199), kind=kCustom, calls=%fused_computation.1 | custom fusion | bytes 147456 | tf_op jit(solution)/shard_map/jit(take_along_axis)/gather | solution.py:44
  116.4 4.7 copy.92
  122.3 17.7 %all_to_all.27 = s32[32,1,384]{2,1,0:T(1,128)S(1)} all-to-all(s32[32,1,384]{2,1,0:T(1,128)S(1)} %reshape.391), channel_id=1, replica_groups=mesh['ctx'=32,'wsh'=8] {'ctx'}, dimensions={0} | all-to-all | bytes 98304 | tf_op jit(solution)/shard_map/all_to_all | solution.py:156
  144.6 3.0 sort.34.cloned.1.call-done
  149.4 92.4 %all-gather.6.cloned.1.call-done = bf16[768,2304]{1,0:T(8,128)(2,1)} async-done(((bf16[96,2304]{1,0:T(8,128)(2,1)}), bf16[768,2304]{1,0:T(8,128)(2,1)}) %all-gather.6.cloned.1.call-update) | async-done | bytes 3538960 | tf_op jit(solution)/shard_map/all_gather | solution.py:121
  241.7 5.4 convolution_convert_fusion.3
  247.2 2.8 copy.85
  250.3 2.9 fusion.38
  253.2 6.2 copy.89
  259.4 6.0 all-to-all-start
  266.3 48.9 %gather_fusion.1 = s32[6144]{0:T(1024)S(1)} fusion(s32[12,512]{1,0:T(8,128)S(1)} %bitcast.198, s32[6144]{0:T(1024)S(1)} %reshape.365), kind=kCustom, calls=%fused_computation.clone | custom fusion | bytes 98304 | tf_op jit(solution)/shard_map/jit(take_along_axis)/gather | solution.py:44
  315.2 119.1 %all-to-all-done = bf16[12,192,512]{1,0,2:T(8,128)(2,1)} async-done(((bf16[12,192,512]{1,0,2:T(8,128)(2,1)}), bf16[12,192,512]{1,0,2:T(8,128)(2,1)}, u32[]{:S(2)}, u32[]{:S(2)}) %all-to-all-start) | async-done | bytes 2359328 | tf_op jit(solution)/shard_map/all_to_all | solution.py:155
  434.4 7.2 fusion.32
  441.5 4.2 reshape.317
  446.8 3.1 fusion.26
  451.3 2.7 fusion.57
  454.0 4.6 fusion.48
  458.6 3.8 copy.101
  462.5 4.3 reshape.393
  466.8 6.2 all-to-all-start.2
  473.6 111.0 %psum.14 = f32[]{:T(128)} all-reduce(f32[]{:T(128)} %convert_reduce_fusion), channel_id=1, replica_groups=mesh['ctx'=32,'wsh'=8] {'ctx','wsh'}, use_global_device_ids=true, to_apply=%region_13.15 | all-reduce | flops 1 | bytes 8 | tf_op jit(solution)/shard_map/psum | solution.py:186
  584.7 23.1 %all-gather = bf16[8,96,4]{1,2,0:T(4,128)(2,1)S(1)} all-gather(bf16[1,96,4]{1,2,0:T(4,128)(2,1)S(1)} %bitcast.230), channel_id=1, replica_groups=mesh['ctx'=32,'wsh'=8] {'wsh'}, dimensions={0}, use_global_device_ids=true | all-gather | bytes 6912 | tf_op jit(solution)/shard_map/all_gather | solution.py:125
  608.7 4.2 reshape.394
  612.9 5.1 fusion.49
  618.0 2.6 fusion.105
  622.1 20.8 %multiply_convert_fusion = (bf16[512,3072]{1,0:T(8,128)(2,1)}, f32[512,3072]{1,0:T(8,128)}, f32[512,3072]{1,0:T(8,128)}) fusion(bf16[768,3072]{1,0:T(8,128)(2,1)} %all-gather.10.cloned.1.call-done, f32[512,768]{1,0:T(8,128)} %copy-done.3, f32[768]{0:T(1024)S(1)} %get-tuple-element.56, f32[768]{0:T(1024)S(1)} %get-tuple-element.57, ...), kind=kOutput, calls=%fused_computation.18 | convolution fusion | flops 2520121344 | bytes 22030336 | tf_op jit(solution)/shard_map/dot_general | solution.py:178
  643.1 6.6 fusion.106
  650.0 2.1 multiply_reduce_fusion.1
  652.1 9.0 add_convert_fusion
  661.1 5.4 multiply_reduce_fusion.2
  668.2 1.9 convolution_convert_fusion.4
  670.2 7.3 convolution_convert_fusion.1
  678.0 7.9 convolution_convert_fusion
  685.9 3.4 convolution_convert_fusion.5
  689.3 2.4 copy.104
  691.7 4.6 fusion.44
  696.3 3.8 copy.105
  700.0 4.3 reshape.395
  704.3 30.5 %all_to_all.28 = bf16[32,2,6144]{2,1,0:T(2,128)(2,1)} all-to-all(bf16[32,2,6144]{2,1,0:T(2,128)(2,1)} %reshape.395), channel_id=1, replica_groups=mesh['ctx'=32,'wsh'=8] {'ctx'}, dimensions={0} | all-to-all | bytes 1572864 | tf_op jit(solution)/shard_map/all_to_all | solution.py:214
  734.8 4.2 reshape.396
  739.0 4.3 fusion.54
  743.3 1.8 fusion.58
  745.3 3.1 multiply_reduce_fusion
  752.6 3.1 fusion.39
  755.7 6.2 copy.115
  761.9 5.3 all-to-all-start.4
  767.2 46.4 %reduce-scatter.21.cloned.1.call-done = bf16[768,24]{0,1:T(8,128)(2,1)} async-done(((bf16[768,768]{0,1:T(8,128)(2,1)}), bf16[768,24]{0,1:T(8,128)(2,1)}) %reduce-scatter.21.cloned.1.call-update) | async-done | bytes 36880 | tf_op jit(solution)/shard_map/reduce_scatter | solution.py:241
  815.5 51.3 %all-to-all-done.4 = bf16[12,192,512]{1,0,2:T(8,128)(2,1)} async-done(((bf16[12,192,512]{1,0,2:T(8,128)(2,1)}), bf16[12,192,512]{1,0,2:T(8,128)(2,1)}, u32[]{:S(2)}, u32[]{:S(2)}) %all-to-all-start.4) | async-done | bytes 2359328 | tf_op jit(solution)/shard_map/all_to_all | solution.py:225
  866.8 5.8 fusion.35
  874.3 3.8 fusion.22
  878.1 89.6 %reduce-scatter.23.cloned.1.call-done = bf16[768,96]{0,1:T(8,128)(2,1)} async-done(((bf16[768,3072]{0,1:T(8,128)(2,1)}), bf16[768,96]{0,1:T(8,128)(2,1)}) %reduce-scatter.23.cloned.1.call-update) | async-done | bytes 147472 | tf_op jit(solution)/shard_map/reduce_scatter | solution.py:244
  967.7 1.7 copy.127
  972.6 80.9 %psum.15 = f32[]{:T(128)} all-reduce(f32[]{:T(128)} %multiply_reduce_fusion.12), channel_id=1, replica_groups=mesh['ctx'=32,'wsh'=8] {'ctx','wsh'}, use_global_device_ids=true, to_apply=%region_21.23 | all-reduce | flops 1 | bytes 8 | tf_op jit(solution)/shard_map/psum | solution.py:186
  1054.9 63.3 %reduce-scatter.25.cloned.1.call-done = bf16[3072,24]{0,1:T(8,128)(2,1)} async-done(((bf16[3072,768]{0,1:T(8,128)(2,1)}), bf16[3072,24]{0,1:T(8,128)(2,1)}) %reduce-scatter.25.cloned.1.call-update) | async-done | bytes 147472 | tf_op jit(solution)/shard_map/reduce_scatter | solution.py:247
  1118.3 2.1 copy.129
  1120.4 73.8 %all-reduce = bf16[4,768]{1,0:T(4,128)(2,1)S(1)} all-reduce(bf16[4,768]{1,0:T(4,128)(2,1)S(1)} %pad_maximum_fusion), channel_id=10, replica_groups=mesh['ctx'=32,'wsh'=8] {'ctx'}, use_global_device_ids=true, to_apply=%region_34.36.clone | all-reduce | flops 3072 | bytes 12288
  1194.4 24.9 %all-reduce.1 = bf16[4,24]{1,0:T(4,128)(2,1)S(1)} all-reduce(bf16[4,24]{1,0:T(4,128)(2,1)S(1)} %constant_dynamic-slice_fusion), channel_id=11, replica_groups=mesh['ctx'=32,'wsh'=8] {'wsh'}, use_global_device_ids=true, to_apply=%region_35.37.clone | all-reduce | flops 96 | bytes 384
  1221.4 129.2 %reduce-scatter.19.cloned.1.call-done = bf16[768,72]{0,1:T(8,128)(2,1)} async-done(((bf16[768,2304]{0,1:T(8,128)(2,1)}), bf16[768,72]{0,1:T(8,128)(2,1)}) %reduce-scatter.19.cloned.1.call-update) | async-done | bytes 110608 | tf_op jit(solution)/shard_map/reduce_scatter | solution.py:238
  1352.3 5.9 add_bitcast_fusion
  1358.2 79.1 %reduce-scatter.31.cloned.1.call-done = bf16[96,96]{1,0:T(8,128)(2,1)} async-done(((bf16[768,96]{1,0:T(8,128)(2,1)}), bf16[96,96]{1,0:T(8,128)(2,1)}) %reduce-scatter.31.cloned.1.call-update) | async-done | bytes 18448
  1438.9 84.4 %reduce-scatter.33.cloned.1.call-done = bf16[384,24]{1,0:T(8,128)(2,1)} async-done(((bf16[3072,24]{1,0:T(8,128)(2,1)}), bf16[384,24]{1,0:T(8,128)(2,1)}) %reduce-scatter.33.cloned.1.call-update) | async-done | bytes 18448
  1524.9 80.8 %reduce-scatter.27.cloned.1.call-done = bf16[96,72]{1,0:T(8,128)(2,1)} async-done(((bf16[768,72]{1,0:T(8,128)(2,1)}), bf16[96,72]{1,0:T(8,128)(2,1)}) %reduce-scatter.27.cloned.1.call-update) | async-done | bytes 13840
  (183 shorter events, 39.1 us)
Async XLA Ops:
  8.0 17.3 %copy-start.20 = (s32[2]{0:T(128)S(1)}, s32[2]{0:T(128)}, u32[]{:S(2)}) copy-start(s32[2]{0:T(128)} %constant.149) | copy-start | bytes 28
  8.0 17.5 %copy-start.19 = (s32[2]{0:T(128)S(1)}, s32[2]{0:T(128)}, u32[]{:S(2)}) copy-start(s32[2]{0:T(128)} %constant.146) | copy-start | bytes 28
  8.0 17.1 %copy-start.14 = (s32[1,12,512]{2,0,1:T(1,128)S(1)}, s32[1,12,512]{2,0,1:T(1,128)}, u32[]{:S(2)}) copy-start(s32[1,12,512]{2,0,1:T(1,128)} %param.14) | copy-start | bytes 73732
  8.0 40.9 %copy-start.17 = (s32[1,512]{1,0:T(1,128)S(1)}, s32[1,512]{1,0:T(1,128)}, u32[]{:S(2)}) copy-start(s32[1,512]{1,0:T(1,128)} %param.15) | copy-start | bytes 6148
  8.0 139.5 %sort.34.cloned.1.call-start = ((), (), s32[]{:S(2)}) async-start(), calls=%async_computation.25 | async-start | bytes 196640 | tf_op jit(solution)/shard_map/jit(argsort)/sort | solution.py:50
  121.2 120.6 %copy-start.21 = (bf16[1,512,768]{2,1,0:T(8,128)(2,1)S(1)}, bf16[1,512,768]{2,1,0:T(8,128)(2,1)}, u32[]{:S(2)}) copy-start(bf16[1,512,768]{2,1,0:T(8,128)(2,1)} %param.12) | copy-start | bytes 2359300
  143.9 97.8 %all-gather.6.cloned.1.call-start = ((), (), s32[]{:S(2)}) async-start(), calls=%async_computation.13 | async-start | bytes 3981312 | tf_op jit(solution)/shard_map/all_gather | solution.py:121
  144.5 309.5 %sort.36.cloned.1.call-start = ((), (), s32[]{:S(2)}) async-start(), calls=%async_computation.26 | async-start | bytes 196640 | tf_op jit(solution)/shard_map/jit(argsort)/sort | solution.py:51
  148.2 469.8 %all-gather.8.cloned.1.call-start = ((), (), s32[]{:S(2)}) async-start(), calls=%async_computation.14 | async-start | bytes 1327104 | tf_op jit(solution)/shard_map/all_gather | solution.py:122
  148.8 473.3 %all-gather.10.cloned.1.call-start = ((), (), s32[]{:S(2)}) async-start(), calls=%async_computation.15 | async-start | bytes 5308416 | tf_op jit(solution)/shard_map/all_gather | solution.py:123
  259.4 6.8 copy-start.15
  259.4 175.0 %all-to-all-start = ((bf16[12,192,512]{1,0,2:T(8,128)(2,1)}), bf16[12,192,512]{1,0,2:T(8,128)(2,1)}, u32[]{:S(2)}, u32[]{:S(2)}) async-start(bf16[12,192,512]{1,0,2:T(8,128)(2,1)} %copy.89), calls=%async_computation | async-start | bytes 8388608 | tf_op jit(solution)/shard_map/all_to_all | solution.py:155
  265.4 377.6 %all-gather.12.cloned.1.call-start = ((), (), s32[]{:S(2)}) async-start(), calls=%async_computation.16 | async-start | bytes 5308416 | tf_op jit(solution)/shard_map/all_gather | solution.py:124
  446.7 4.5 copy-start.5
  446.7 4.5 copy-start.7
  446.7 4.6 copy-start.10
  458.6 14.4 copy-start.16
  458.6 126.0 %copy-start.18 = (bf16[4,96]{1,0:T(4,128)(2,1)S(1)}, bf16[4,96]{1,0:T(4,128)(2,1)}, u32[]{:S(2)}) copy-start(bf16[4,96]{1,0:T(4,128)(2,1)} %param.21) | copy-start | bytes 2308
  466.8 141.9 %all-to-all-start.2 = ((bf16[32,2,6144]{2,1,0:T(2,128)(2,1)}), bf16[32,2,6144]{2,1,0:T(2,128)(2,1)}, u32[]{:S(2)}, u32[]{:S(2)}) async-start(bf16[32,2,6144]{2,1,0:T(2,128)(2,1)} %reshape.393), calls=%async_computation.2 | async-start | bytes 1572864 | tf_op jit(solution)/shard_map/all_to_all | solution.py:164
  473.0 340.6 %reduce-scatter.21.cloned.1.call-start = ((), (), s32[]{:S(2)}) async-start(), calls=%async_computation.18 | async-start | bytes 1216512 | tf_op jit(solution)/shard_map/reduce_scatter | solution.py:241
  620.7 1.1 copy-start.3
  643.0 9.0 slice-start.2
  643.0 7.0 copy-start.13
  643.0 9.0 slice-start.3
  649.7 11.5 copy-start.2
  650.0 11.1 slice-start
  652.1 9.0 copy-start.4
  652.1 9.0 slice-start.1
  666.5 1.7 copy-start.12
  667.0 1.2 copy-start
  670.1 297.6 %reduce-scatter.23.cloned.1.call-start = ((), (), s32[]{:S(2)}) async-start(), calls=%async_computation.19 | async-start | bytes 4866048 | tf_op jit(solution)/shard_map/reduce_scatter | solution.py:244
  677.5 440.7 %reduce-scatter.25.cloned.1.call-start = ((), (), s32[]{:S(2)}) async-start(), calls=%async_computation.20 | async-start | bytes 4866048 | tf_op jit(solution)/shard_map/reduce_scatter | solution.py:247
  743.3 2.0 copy-start.11
  748.4 1.7 copy-start.8
  750.1 1.1 copy-start.6
  750.7 1.9 copy-start.23
  761.9 104.9 %all-to-all-start.4 = ((bf16[12,192,512]{1,0,2:T(8,128)(2,1)}), bf16[12,192,512]{1,0,2:T(8,128)(2,1)}, u32[]{:S(2)}, u32[]{:S(2)}) async-start(bf16[12,192,512]{1,0,2:T(8,128)(2,1)} %copy.115), calls=%async_computation.4 | async-start | bytes 8388608 | tf_op jit(solution)/shard_map/all_to_all | solution.py:225
  767.2 452.8 %reduce-scatter.29.cloned.1.call-start = ((), (), s32[]{:S(2)}) async-start(), calls=%async_computation.22 | async-start | bytes 221184
  815.2 535.4 %reduce-scatter.19.cloned.1.call-start = ((), (), s32[]{:S(2)}) async-start(), calls=%async_computation.17 | async-start | bytes 3649536 | tf_op jit(solution)/shard_map/reduce_scatter | solution.py:238
  872.6 1.7 copy-start.22
  872.9 1.4 copy-start.9
  878.1 91.5 %copy-start.25 = (u32[256]{0:T(256)S(1)}, u32[256]{0:T(256)}, u32[]{:S(2)}) copy-start(u32[256]{0:T(256)} %constant.192) | copy-start | bytes 3076
  878.1 92.1 %copy-start.24 = (u32[256]{0:T(256)S(1)}, u32[256]{0:T(256)}, u32[]{:S(2)}) copy-start(u32[256]{0:T(256)} %constant.188) | copy-start | bytes 3076
  878.1 474.3 %copy-start.1 = (f32[512,768]{1,0:T(8,128)S(1)}, f32[512,768]{1,0:T(8,128)}, u32[]{:S(2)}) copy-start(f32[512,768]{1,0:T(8,128)} %copy-done) | copy-start | bytes 4718596
  878.1 559.3 %reduce-scatter.31.cloned.1.call-start = ((), (), s32[]{:S(2)}) async-start(), calls=%async_computation.23 | async-start | bytes 221184
  969.5 553.8 %reduce-scatter.33.cloned.1.call-start = ((), (), s32[]{:S(2)}) async-start(), calls=%async_computation.24 | async-start | bytes 884736
  1120.4 485.3 %reduce-scatter.27.cloned.1.call-start = ((), (), s32[]{:S(2)}) async-start(), calls=%async_computation.21 | async-start | bytes 221184
Sparse Core Ops, SparseCore 0:
  144.1 3.2 sort.38.cloned.1.call-done
  150.7 3.4 sort.40.cloned.1.call-done
  670.2 143.3 reduce-scatter.20
  816.2 151.5 reduce-scatter.22
  970.3 147.9 reduce-scatter.24
  1123.0 82.5 reduce-scatter.28
  1208.1 142.4 reduce-scatter.18
  1355.0 82.3 reduce-scatter.30
  1441.3 81.9 reduce-scatter.32
  1527.0 78.6 reduce-scatter.26
  (2 shorter events, 0.0 us)
Sparse Core Ops, SparseCore 1:
  147.0 94.6 all-gather.5
  244.2 59.6 all-gather.7
  306.4 130.7 all-gather.9
  439.7 100.6 all-gather.11
where the time goes:
time: 1630 us; the launch traced here: 1620 us
  waiting for transfers between devices  837 us (51%)
  blocking collectives  362 us (22%)
  local copies, waits for them, and re-layouts  218 us (13%)
  matrix products  130 us (8%)
  other arithmetic  28.1 us (2%)
  between operations  21.5 us (1%)
  starting transfers between devices  19.2 us (1%)
    unnamed x16, waiting for transfers between devices  246 us
    psum x2, blocking collectives, local(): lax.psum((partial_value, jnp.sum(mask_rows)), ('ctx', 'wsh'))  192 us
    reduce_scatter x1, waiting for transfers between devices, local(): lax.psum_scatter(grad_inw.astype(jnp.bfloat16), 'ctx', scatter_dimension=...  129 us
    gather x5, local copies, waits for them, and re-layouts, take_index(): return jnp.take_along_axis(array, index[:, None, :], axis=2)  120 us
    all_to_all x1, waiting for transfers between devices, local(): lax.all_to_all(sent_qkv, 'ctx', split_axis=2, concat_axis=2, tiled=True)  119 us
    unnamed x2, blocking collectives  98.8 us
    all_gather x1, waiting for transfers between devices, local(): lax.all_gather(w_qkv, 'wsh', axis=0, tiled=True)  92.4 us
    reduce_scatter x1, waiting for transfers between devices, local(): lax.psum_scatter(grad_up.astype(jnp.bfloat16), 'ctx', scatter_dimension=1...  89.6 us
  transfers between devices with their start and end apart: 15, of which 10 were waited for; matrix products, arithmetic and copies ran while one was open for 14% of the time, Pallas kernels for 0%

commit v1 on v0

--- a/solution.py
+++ b/solution.py
@@ -1,9 +1,481 @@
+import functools
 import jax
 import jax.numpy as jnp
 from jax import lax
+from jax.experimental import pallas as pl
+from jax.experimental.pallas import tpu as pltpu
 from jax.sharding import PartitionSpec as P
 
 CLUSTER = 128
+MESH = pl.DeviceIdType.MESH
+BF16 = jnp.bfloat16
+F32 = jnp.float32
+
+
+class Place:
+    def __init__(self):
+        self.ctx = lax.axis_index("ctx")
+        self.wsh = lax.axis_index("wsh")
+        self.zlo = self.ctx // 8
+        self.y = (self.ctx // 2) % 4
+        self.core = self.ctx % 2
+        self.zhi = self.wsh // 4
+        self.x = self.wsh % 4
+
+    def at(self, zlo=None, y=None, core=None, zhi=None, x=None):
+        zlo = self.zlo if zlo is None else zlo
+        y = self.y if y is None else y
+        core = self.core if core is None else core
+        zhi = self.zhi if zhi is None else zhi
+        x = self.x if x is None else x
+        return (zlo * 8 + y * 2 + core, zhi * 4 + x)
+
+    def sibling(self):
+        return self.at(core=1 - self.core)
+
+    def x_peer(self, step):
+        return self.at(x=(self.x + step) % 4)
+
+    def y_peer(self, step):
+        return self.at(y=(self.y + step) % 4)
+
+    def z_far(self):
+        return self.at(zhi=1 - self.zhi)
+
+    def doubling(self):
+        return (
+            self.sibling(),
+            self.at(y=self.y + 1 - 2 * (self.y % 2)),
+            self.at(y=(self.y + 2) % 4),
+            self.at(x=self.x + 1 - 2 * (self.x % 2)),
+            self.at(x=(self.x + 2) % 4),
+            self.at(zlo=self.zlo + 1 - 2 * (self.zlo % 2)),
+            self.at(zlo=(self.zlo + 2) % 4),
+            self.z_far(),
+        )
+
+
+def greet(devices):
+    barrier = pltpu.get_barrier_semaphore()
+    for device in devices:
+        pl.semaphore_signal(barrier, inc=1, device_id=device, device_id_type=MESH)
+    pl.semaphore_wait(barrier, len(devices))
+
+
+def remote(source, target, send_sem, recv_sem, device):
+    return pltpu.make_async_remote_copy(
+        src_ref=source,
+        dst_ref=target,
+        send_sem=send_sem,
+        recv_sem=recv_sem,
+        device_id=device,
+        device_id_type=MESH,
+    )
+
+
+def half_of(width, which):
+    half = width // 2
+    return pl.ds(pl.multiple_of(which * half, 128), half)
+
+
+class Doubling:
+    def __init__(self, place, tile, slots, send_sems, recv_sems):
+        self.partners = place.doubling()
+        self.tile, self.slots = tile, slots
+        self.send_sems, self.recv_sems = send_sems, recv_sems
+        self.step = 0
+        self.copies = []
+
+    def start(self):
+        k = self.step
+        copy = remote(
+            self.tile.at[k], self.slots.at[k], self.send_sems.at[k], self.recv_sems.at[k], self.partners[k]
+        )
+        copy.start()
+        self.copies.append(copy)
+
+    def advance(self):
+        k = self.step
+        self.copies[k].wait_recv()
+        self.tile[k + 1] = self.tile[k] + self.slots[k]
+        self.step = k + 1
+        if self.step < 8:
+            self.start()
+
+    def drain(self):
+        for copy in self.copies:
+            copy.wait_send()
+
+
+def gather_kernel(
+    wq, wo, wu, wd, wn, count, fq, fo, fu, fd, fn, total,
+    tile, slots, send_sem, recv_sem, local_sem, tile_send, tile_recv,
+):
+    place = Place()
+    own, far = place.wsh, (1 - place.zhi) * 4 + place.x
+    greet(
+        [place.x_peer(d) for d in (1, 2, 3)]
+        + [place.z_far(), place.sibling()]
+        + [place.doubling()[k] for k in (1, 2, 5, 6)]
+    )
+    arrays = ((wq, fq), (wo, fo), (wu, fu), (wd, fd), (wn, fn))
+    tile[0] = count[...]
+    doubling = Doubling(place, tile, slots, tile_send, tile_recv)
+    doubling.start()
+    sends = []
+
+    def half(ref, which):
+        width = ref.shape[-1]
+        if width < 256:
+            return ref
+        return ref.at[:, half_of(width, which)]
+
+    locals_ = []
+    first = []
+    for i, (shard, full) in enumerate(arrays):
+        copy = pltpu.make_async_copy(shard, full.at[own], local_sem.at[i])
+        copy.start()
+        locals_.append(copy)
+        copies = []
+        for k, device in enumerate([place.x_peer(d) for d in (1, 2, 3)] + [place.z_far()]):
+            copies.append(
+                remote(
+                    half(shard, place.core), half(full.at[own], place.core),
+                    send_sem.at[i, k], recv_sem.at[i, k], device,
+                )
+            )
+            copies[-1].start()
+        first.append(copies)
+    forwards = []
+
+    def forward(i, k, index):
+        shard, full = arrays[i]
+        if shard.shape[-1] < 256:
+            return
+        part = half(full.at[index], place.core)
+        copy = remote(part, part, send_sem.at[i, 7 + k], recv_sem.at[i, 7 + k], place.sibling())
+        copy.start()
+        forwards.append(copy)
+
+    second = []
+    for i, (shard, full) in enumerate(arrays):
+        first[i][3].wait_recv()
+        copies = []
+        for k, d in enumerate((1, 2, 3)):
+            part = half(full.at[far], place.core)
+            copies.append(
+                remote(part, part, send_sem.at[i, 4 + k], recv_sem.at[i, 4 + k], place.x_peer(d))
+            )
+            copies[-1].start()
+        second.append(copies)
+        forward(i, 3, far)
+        if i < 4:
+            doubling.advance()
+    for i in range(5):
+        for k, d in enumerate((1, 2, 3)):
+            first[i][k].wait_recv()
+            forward(i, k, place.zhi * 4 + (place.x - d + 4) % 4)
+        if i < 4:
+            doubling.advance()
+    for i in range(5):
+        for k, d in enumerate((1, 2, 3)):
+            second[i][k].wait_recv()
+            forward(i, 4 + k, (1 - place.zhi) * 4 + (place.x - d + 4) % 4)
+    total[...] = tile[8]
+    for copy in forwards:
+        copy.wait_recv()
+    for copy in forwards + sum(first, []) + sum(second, []):
+        copy.wait_send()
+    for copy in locals_:
+        copy.wait()
+    doubling.drain()
+
+
+def gather_weights(w_qkv, w_out, w_up, w_down, norms, counted):
+    any_space = pl.BlockSpec(memory_space=pl.ANY)
+    vmem = pl.BlockSpec(memory_space=pltpu.VMEM)
+    tile_norms = jnp.zeros((16, 128), BF16).at[: norms.shape[0], : norms.shape[1]].set(norms)
+    count = jnp.broadcast_to(jnp.sum(counted.astype(F32)), (8, 128))
+    shards = (w_qkv, w_out, w_up, w_down, tile_norms)
+    fq, fo, fu, fd, fn, total = pl.pallas_call(
+        gather_kernel,
+        out_shape=[jax.ShapeDtypeStruct((8, *w.shape), BF16) for w in shards]
+        + [jax.ShapeDtypeStruct((8, 128), F32)],
+        in_specs=[any_space] * 5 + [vmem],
+        out_specs=[any_space] * 5 + [vmem],
+        scratch_shapes=[
+            pltpu.VMEM((9, 8, 128), F32),
+            pltpu.VMEM((8, 8, 128), F32),
+            pltpu.SemaphoreType.DMA((5, 14)),
+            pltpu.SemaphoreType.DMA((5, 14)),
+            pltpu.SemaphoreType.DMA((5,)),
+            pltpu.SemaphoreType.DMA((8,)),
+            pltpu.SemaphoreType.DMA((8,)),
+        ],
+        compiler_params=pltpu.CompilerParams(collective_id=0, has_side_effects=True),
+        name="gather_weights",
+    )(*shards, count)
+    full_norms = fn[:, : norms.shape[0], : norms.shape[1]].transpose(1, 0, 2).reshape(norms.shape[0], -1)
+    return (
+        fq.reshape(-1, fq.shape[-1]),
+        fo.reshape(-1, fo.shape[-1]),
+        fu.reshape(-1, fu.shape[-1]),
+        fd.reshape(-1, fd.shape[-1]),
+        full_norms,
+        total[0, 0],
+    )
+
+
+def reduce_kernel(*refs):
+    gq, go, gu, gd, small = refs[:5]
+    outs, small_out = refs[5:9], refs[9]
+    held, from_x, sum_x, from_y, sum_y, from_z = (refs[10 + 4 * k : 14 + 4 * k] for k in range(6))
+    tile, slots, send_sem, recv_sem, tile_send, tile_recv = refs[34:]
+    grads = (gq, go, gu, gd)
+    place = Place()
+    near_z = (place.doubling()[5], place.doubling()[6])
+    plane = [
+        place.at(y=(place.y + d) % 4, core=(place.core + c) % 2)
+        for d in range(4)
+        for c in range(2)
+        if d + c > 0
+    ]
+    greet(plane + [place.x_peer(d) for d in (1, 2, 3)] + [place.z_far(), *near_z])
+    tile[0] = small[...]
+    doubling = Doubling(place, tile, slots, tile_send, tile_recv)
+    doubling.start()
+    sends = []
+
+    def go_on(copy):
+        copy.start()
+        sends.append(copy)
+        return copy
+
+    pair = []
+    for i, grad in enumerate(grads):
+        width = grad.shape[-1]
+        pair.append(
+            go_on(
+                remote(
+                    grad.at[:, :, :, half_of(width, 1 - place.core)], held[i],
+                    send_sem.at[i, 0], recv_sem.at[i, 0], place.sibling(),
+                )
+            )
+        )
+    doubling.advance()
+    across = []
+    for i, grad in enumerate(grads):
+        width, rows = grad.shape[-1], grad.shape[2]
+        pair[i].wait_recv()
+        lanes = half_of(width, place.core)
+
+        def add_pair(step, carry, grad=grad, i=i, lanes=lanes, rows=rows):
+            block = step // (rows // 48)
+            zh, xx = block // 4, block % 4
+            part = pl.ds(pl.multiple_of((step % (rows // 48)) * 48, 16), 48)
+            mine = grad[zh, xx, part, lanes].astype(F32)
+            held[i][zh, xx, part, :] = (mine + held[i][zh, xx, part, :].astype(F32)).astype(BF16)
+            return carry
+
+        lax.fori_loop(0, 8 * (rows // 48), add_pair, 0)
+        copies = []
+        for k, d in enumerate((1, 2, 3)):
+            to = (place.x + d) % 4
+            copies.append(
+                go_on(
+                    remote(
+                        held[i].at[:, to], from_x[i].at[k],
+                        send_sem.at[i, 1 + k], recv_sem.at[i, 1 + k], place.x_peer(d),
+                    )
+                )
+            )
+        across.append(copies)
+    doubling.advance()
+    along = []
+    for i, grad in enumerate(grads):
+        rows = grad.shape[2]
+        for copy in across[i]:
+            copy.wait_recv()
+
+        def add_x(step, carry, i=i, rows=rows):
+            zh = step // (rows // 48)
+            part = pl.ds(pl.multiple_of((step % (rows // 48)) * 48, 16), 48)
+            value = held[i][zh, place.x, part, :].astype(F32)
+            for k in range(3):
+                value = value + from_x[i][k, zh, part, :].astype(F32)
+            sum_x[i][zh, part, :] = value.astype(BF16)
+            return carry
+
+        lax.fori_loop(0, 2 * (rows // 48), add_x, 0)
+        copies = []
+        for k, d in enumerate((1, 2, 3)):
+            to = (place.y + d) % 4
+            part = pl.ds(pl.multiple_of((to % 2) * (rows // 2), 16), rows // 2)
+            copies.append(
+                go_on(
+                    remote(
+                        sum_x[i].at[to // 2, part], from_y[i].at[k],
+                        send_sem.at[i, 4 + k], recv_sem.at[i, 4 + k], place.y_peer(d),
+                    )
+                )
+            )
+        along.append(copies)
+        doubling.advance()
+    owner = place.y // 2
+    side = place.zlo // 2
+    here = place.zhi == owner
+    mine = jnp.logical_and(here, place.core == side)
+    other = jnp.logical_and(here, place.core != side)
+
+    def z_copy(i, k, device):
+        return remote(sum_y[i], from_z[i].at[k], send_sem.at[i, 7 + k], recv_sem.at[i, 7 + k], device)
+
+    def add_z(i, k):
+        rows = sum_y[i].shape[0]
+
+        def body(step, carry):
+            part = pl.ds(pl.multiple_of(step * 48, 16), 48)
+            sum_y[i][part, :] = (
+                sum_y[i][part, :].astype(F32) + from_z[i][k, part, :].astype(F32)
+            ).astype(BF16)
+            return carry
+
+        lax.fori_loop(0, rows // 48, body, 0)
+
+    for i, grad in enumerate(grads):
+        rows = grad.shape[2]
+        for copy in along[i]:
+            copy.wait_recv()
+
+        def add_y(step, carry, i=i, rows=rows):
+            part = pl.ds(pl.multiple_of((place.y % 2) * (rows // 2) + step * 48, 16), 48)
+            value = sum_x[i][owner, part, :].astype(F32)
+            there = pl.ds(pl.multiple_of(step * 48, 16), 48)
+            for k in range(3):
+                value = value + from_y[i][k, there, :].astype(F32)
+            sum_y[i][there, :] = value.astype(BF16)
+            return carry
+
+        lax.fori_loop(0, rows // 96, add_y, 0)
+
+        @pl.when(jnp.logical_not(here))
+        def _(i=i):
+            z_copy(i, 0, place.z_far()).start()
+
+    doubling.advance()
+    for i in range(4):
+        @pl.when(here)
+        def _(i=i):
+            z_copy(i, 0, place.z_far()).wait_recv()
+            add_z(i, 0)
+
+        @pl.when(other)
+        def _(i=i):
+            z_copy(i, 1, near_z[1]).start()
+
+    doubling.advance()
+    for i in range(4):
+        @pl.when(mine)
+        def _(i=i):
+            z_copy(i, 1, near_z[1]).wait_recv()
+            add_z(i, 1)
+            z_copy(i, 2, near_z[0]).start()
+
+    def cast_copy(i, k, device):
+        rows = sum_y[i].shape[0]
+        part = pl.ds(pl.multiple_of((place.y % 2) * rows, 16), rows)
+        return remote(
+            outs[i].at[part], outs[i].at[part],
+            send_sem.at[i, 10 + k], recv_sem.at[i, 10 + place.y % 2], device,
+        )
+
+    for i in range(4):
+        @pl.when(mine)
+        def _(i=i):
+            copy = z_copy(i, 2, near_z[0])
+            copy.wait()
+            rows = sum_y[i].shape[0]
+
+            def body(step, carry):
+                part = pl.ds(pl.multiple_of(step * 48, 16), 48)
+                there = pl.ds(pl.multiple_of((place.y % 2) * rows + step * 48, 16), 48)
+                outs[i][there, :] = (
+                    sum_y[i][part, :].astype(F32) + from_z[i][2, part, :].astype(F32)
+                ).astype(BF16)
+                return carry
+
+            lax.fori_loop(0, rows // 48, body, 0)
+            for k, device in enumerate(plane):
+                cast_copy(i, k, device).start()
+
+    def arrived(i, k):
+        rows = sum_y[i].shape[0]
+        part = outs[i].at[pl.ds(k * rows, rows)]
+        return remote(part, part, send_sem.at[i, 10], recv_sem.at[i, 10 + k], place.sibling())
+
+    for i in range(4):
+        for k in range(2):
+            @pl.when(jnp.logical_not(jnp.logical_and(mine, place.y % 2 == k)))
+            def _(i=i, k=k):
+                arrived(i, k).wait_recv()
+
+    small_out[...] = tile[8]
+    for i in range(4):
+        @pl.when(mine)
+        def _(i=i):
+            for k, device in enumerate(plane):
+                cast_copy(i, k, device).wait_send()
+
+        @pl.when(other)
+        def _(i=i):
+            z_copy(i, 1, near_z[1]).wait_send()
+
+        @pl.when(jnp.logical_not(here))
+        def _(i=i):
+            z_copy(i, 0, place.z_far()).wait_send()
+
+    for copy in sends:
+        copy.wait_send()
+    doubling.drain()
+
+
+def reduce_grads(grads, small):
+    vmem = pl.BlockSpec(memory_space=pltpu.VMEM)
+    blocks = [g.reshape(2, 4, g.shape[0] // 8, g.shape[1]) for g in grads]
+    rows = [b.shape[2] for b in blocks]
+    half = [b.shape[3] // 2 for b in blocks]
+    each = lambda shape: [pltpu.VMEM(shape(r, h), BF16) for r, h in zip(rows, half)]
+    results = pl.pallas_call(
+        reduce_kernel,
+        out_shape=[jax.ShapeDtypeStruct((r, h), BF16) for r, h in zip(rows, half)]
+        + [jax.ShapeDtypeStruct(small.shape, F32)],
+        in_specs=[vmem] * 5,
+        out_specs=[vmem] * 5,
+        scratch_shapes=each(lambda r, h: (2, 4, r, h))
+        + each(lambda r, h: (3, 2, r, h))
+        + each(lambda r, h: (2, r, h))
+        + each(lambda r, h: (3, r // 2, h))
+        + each(lambda r, h: (r // 2, h))
+        + each(lambda r, h: (3, r // 2, h))
+        + [
+            pltpu.VMEM((9, *small.shape), F32),
+            pltpu.VMEM((8, *small.shape), F32),
+            pltpu.SemaphoreType.DMA((4, 17)),
+            pltpu.SemaphoreType.DMA((4, 17)),
+            pltpu.SemaphoreType.DMA((8,)),
+            pltpu.SemaphoreType.DMA((8,)),
+        ],
+        compiler_params=pltpu.CompilerParams(
+            collective_id=1, has_side_effects=True, vmem_limit_bytes=60 * 2**20
+        ),
+        name="reduce_grads",
+    )(*blocks, small)
+    ctx = lax.axis_index("ctx")
+    finals = []
+    for result in results[:4]:
+        width = result.shape[1] // 16
+        finals.append(lax.dynamic_slice_in_dim(result, (ctx % 16) * width, width, axis=1).astype(F32))
+    return finals, results[4]
 
 
 def layer_norm(values, gain_row, shift_row):
@@ -117,12 +589,8 @@
 
 
 def local(tokens, teacher, clusters, segments, counted, w_qkv, w_out, w_up, w_down, norms):
-    full_qkv, full_out, full_up, full_down, full_norms = (
-        lax.all_gather(w_qkv, "wsh", axis=0, tiled=True),
-        lax.all_gather(w_out, "wsh", axis=0, tiled=True),
-        lax.all_gather(w_up, "wsh", axis=0, tiled=True),
-        lax.all_gather(w_down, "wsh", axis=0, tiled=True),
-        lax.all_gather(norms, "wsh", axis=1, tiled=True),
+    full_qkv, full_out, full_up, full_down, full_norms, total_count = gather_weights(
+        w_qkv, w_out, w_up, w_down, norms, counted
     )
     x_rows = tokens[0]
     tok_count, model_dim = x_rows.shape
@@ -183,8 +651,6 @@
     errors = result - teacher[0].astype(jnp.float32)
     mask_rows = counted[0].astype(jnp.float32)
     partial_value = jnp.sum(mask_rows * jnp.mean(errors * errors, axis=1))
-    total_error, total_count = lax.psum((partial_value, jnp.sum(mask_rows)), ("ctx", "wsh"))
-    loss_value = total_error / total_count
     everyone = tok_count * peer_count * lax.axis_size("wsh")
     grad_result = everyone / total_count * mask_rows[:, None] * errors
     grad_second, grad_gain_two, grad_shift_two = norm_back(
@@ -210,16 +676,10 @@
     grad_heads = permute(
         grad_mixed.reshape(tok_count, head_count, head_size).transpose(1, 2, 0), send_table
     )
-    grad_got, again_qkv, again_labels = (
-        lax.all_to_all(grad_heads, "ctx", split_axis=2, concat_axis=2, tiled=True),
-        lax.all_to_all(sent_qkv, "ctx", split_axis=2, concat_axis=2, tiled=True),
-        lax.all_to_all(sent_labels, "ctx", split_axis=2, concat_axis=2, tiled=True),
-    )
-    back_order, back_inverse = cluster_order(again_labels)
-    back_table = selector(back_order)
-    back_home = selector(back_inverse)
-    back_blocks = as_blocks(permute(again_qkv, back_table))
-    back_segs = as_blocks(take_index(again_labels[:, 1:2, :], back_order))[:, 0]
+    grad_got = lax.all_to_all(grad_heads, "ctx", split_axis=2, concat_axis=2, tiled=True)
+    back_table = order_table
+    back_home = inverse_table
+    back_blocks, back_segs = qkv_blocks, seg_blocks
     grad_blocks = as_blocks(permute(grad_got, back_table))
     grad_packed = attend_backward(back_blocks, back_segs, logsum, grad_blocks, head_size)
     grad_home = lax.all_to_all(
@@ -234,40 +694,14 @@
     grad_inw = jnp.dot(x_rows.T, grad_qkv, preferred_element_type=jnp.float32)
     grad_tokens = jnp.dot(grad_qkv, full_qkv.T, preferred_element_type=jnp.float32) + grad_first
     grad_norms = jnp.stack([grad_gain_one, grad_shift_one, grad_gain_two, grad_shift_two])
-    part_qkv, part_out, part_up, part_down, part_norms = (
-        lax.psum_scatter(
-            grad_inw.astype(jnp.bfloat16), "ctx", scatter_dimension=1, tiled=True
-        ).astype(jnp.float32),
-        lax.psum_scatter(
-            grad_outw.astype(jnp.bfloat16), "ctx", scatter_dimension=1, tiled=True
-        ).astype(jnp.float32),
-        lax.psum_scatter(
-            grad_up.astype(jnp.bfloat16), "ctx", scatter_dimension=1, tiled=True
-        ).astype(jnp.float32),
-        lax.psum_scatter(
-            grad_down.astype(jnp.bfloat16), "ctx", scatter_dimension=1, tiled=True
-        ).astype(jnp.float32),
-        lax.psum_scatter(
-            grad_norms.astype(jnp.bfloat16), "ctx", scatter_dimension=1, tiled=True
-        ).astype(jnp.float32),
-    )
-    final_qkv, final_out, final_up, final_down, final_norms = (
-        lax.psum_scatter(
-            part_qkv.astype(jnp.bfloat16), "wsh", scatter_dimension=0, tiled=True
-        ).astype(jnp.float32),
-        lax.psum_scatter(
-            part_out.astype(jnp.bfloat16), "wsh", scatter_dimension=0, tiled=True
-        ).astype(jnp.float32),
-        lax.psum_scatter(
-            part_up.astype(jnp.bfloat16), "wsh", scatter_dimension=0, tiled=True
-        ).astype(jnp.float32),
-        lax.psum_scatter(
-            part_down.astype(jnp.bfloat16), "wsh", scatter_dimension=0, tiled=True
-        ).astype(jnp.float32),
-        lax.psum_scatter(
-            part_norms.astype(jnp.bfloat16), "wsh", scatter_dimension=1, tiled=True
-        ).astype(jnp.float32),
-    )
+    small = jnp.zeros((8, model_dim), F32).at[:4].set(grad_norms).at[4, 0].set(partial_value)
+    (final_qkv, final_out, final_up, final_down), small = reduce_grads(
+        [g.astype(BF16) for g in (grad_inw, grad_outw, grad_up, grad_down)], small
+    )
+    loss_value = small[4, 0] / total_count
+    width = model_dim // (peer_count * lax.axis_size("wsh"))
+    at = lax.axis_index("ctx") * lax.axis_size("wsh") + lax.axis_index("wsh")
+    final_norms = lax.dynamic_slice(small, (0, at * width), (4, width))
     return (
         result.astype(jnp.bfloat16)[None],
         grad_tokens[None],

time: 1630 us -> 825 us (0.51)
  waiting for transfers between devices: 837 us -> 130 us
  blocking collectives: 362 us -> 26.3 us
  Pallas kernels: 0 us -> 257 us
    reduce_scatter x4 -> x0, waiting for transfers between devices: 329 us -> none  [the longest x1 129 us: local(): lax.psum_scatter(grad_inw.astype(jnp.bfloat16), 'ctx', scatter_dimension=...]
    pallas_call x0 -> x2, Pallas kernels: none -> 257 us  [the longest x1 152 us: reduce_grads(): pl.pallas_call(reduce_kernel, out_shape=[jax.ShapeDtypeStruct((r, h), BF1...]
    unnamed x16 -> x0, waiting for transfers between devices: 246 us -> none
    psum x2 -> x0, blocking collectives: 192 us -> none  [local(): lax.psum((partial_value, jnp.sum(mask_rows)), ('ctx', 'wsh'))]
    unnamed x2 -> x0, blocking collectives: 98.8 us -> none
    all_gather x4 -> x0, waiting for transfers between devices: 92.4 us -> none  [the longest x1 92.4 us: local(): lax.all_gather(w_qkv, 'wsh', axis=0, tiled=True)]
    all_to_all x1, waiting for transfers between devices: 119 us -> 34.5 us  [local(): lax.all_to_all(sent_qkv, 'ctx', split_axis=2, concat_axis=2, tiled=True)]
    all_to_all x1, waiting for transfers between devices: 51.3 us -> 77.2 us  [local(): lax.all_to_all(permute(from_blocks(grad_packed), back_home), 'ctx', split...]
  transfers between devices with their start and end apart: 15 -> 4, of which waited for: 10 -> 3; matrix products, arithmetic and copies ran while one was open for 14% -> 11% of each run, Pallas kernels for 0% -> 13%
where the time goes in v1:
time: 825 us; the launch traced here: 817 us
  Pallas kernels  257 us (31%)
  local copies, waits for them, and re-layouts  211 us (26%)
  waiting for transfers between devices  130 us (16%)
  matrix products  115 us (14%)
  other arithmetic  32.2 us (4%)
  starting transfers between devices  27.1 us (3%)
  blocking collectives  26.3 us (3%)
  between operations  18.4 us (2%)
    pallas_call x1, Pallas kernels, reduce_grads(): pl.pallas_call(reduce_kernel, out_shape=[jax.ShapeDtypeStruct((r, h), BF1...  152 us
    gather x4, local copies, waits for them, and re-layouts, take_index(): return jnp.take_along_axis(array, index[:, None, :], axis=2)  120 us
    pallas_call x1, Pallas kernels, gather_weights(): pl.pallas_call(gather_kernel, out_shape=[jax.ShapeDtypeStruct((8, *w.shap...  105 us
    all_to_all x1, waiting for transfers between devices, local(): lax.all_to_all(permute(from_blocks(grad_packed), back_home), 'ctx', split...  77.2 us
    unnamed x85, local copies, waits for them, and re-layouts  48.1 us
    dot_general x8, matrix products, permute(): jnp.einsum('hct,hts->hcs', array, table, preferred_element_type=jnp.float32)  36.7 us
    all_to_all x1, waiting for transfers between devices, local(): lax.all_to_all(sent_qkv, 'ctx', split_axis=2, concat_axis=2, tiled=True)  34.5 us
    all_to_all x1, blocking collectives, local(): lax.all_to_all(grad_heads, 'ctx', split_axis=2, concat_axis=2, tiled=True)  26.3 us
  transfers between devices with their start and end apart: 4, of which 3 were waited for; matrix products, arithmetic and copies ran while one was open for 11% of the time, Pallas kernels for 13%

profile of v1, /device:TPU:1, one launch (start us, length us, event | category | flops | bytes accessed | tf_op | source)
XLA Modules:
  0.0 817.4 jit_solution(411120340143558077)
XLA Ops:
  8.9 13.8 %reduce-window.6 = s32[12,32,4,128]{3,1,2,0:T(8,128)S(1)} reduce-window(s32[12,32,4,128]{3,1,2,0:T(8,128)S(1)} %fusion.71, s32[]{:T(128)} %constant.212.clone.1), window={size=1x1x1x128 pad=0_0x0_0x0_0x127_0}, to_apply=%region_1.0 | reduce-window | flops 24969216 | bytes 1572868 | tf_op jit(solution)/shard_map/reduce-window
  22.7 1.1 slice_reduce_fusion
  24.8 23.0 %scatter_custom_fusion = s32[6144]{0:T(1024)S(1)} fusion(s32[6144]{0:T(1024)S(1)} %reshape.513, s32[6144]{0:T(1024)S(1)} %reshape.515, s32[]{:T(128)} %constant.212.clone.1), kind=kCustom, calls=%fused_computation.185 | custom fusion | bytes 24580
  48.0 1.1 copy.60
  49.0 66.4 %gather_fusion = s32[6144,2]{1,0:T(8,128)} fusion(s32[12,2,512]{1,2,0:T(8,128)S(1)} %copy.60, s32[6144]{0:T(1024)S(1)} %reshape.499), kind=kCustom, calls=%fused_computation | custom fusion | bytes 147456 | tf_op jit(solution)/shard_map/jit(take_along_axis)/gather | solution.py:516
  115.4 4.8 copy.61
  120.8 1.4 reshape.557
  122.2 10.5 %all-to-all-start.1 = ((s32[32,1,384]{2,1,0:T(1,128)}), s32[32,1,384]{2,1,0:T(1,128)S(1)}, u32[]{:S(2)}, u32[]{:S(2)}) async-start(s32[32,1,384]{2,1,0:T(1,128)} %reshape.557), calls=%async_computation.1 | async-start | bytes 98304 | tf_op jit(solution)/shard_map/all_to_all | solution.py:624
  133.9 1.2 broadcast_in_dim.35.count
  135.1 104.8 %gather_weights.1 = (bf16[8,96,2304]{2,1,0:T(8,128)(2,1)}, bf16[8,96,768]{2,1,0:T(8,128)(2,1)}, bf16[8,96,3072]{2,1,0:T(8,128)(2,1)}, bf16[8,384,768]{2,1,0:T(8,...) custom-call(bf16[96,2304]{1,0:T(8,128)(2,1)} %wq.1, bf16[96,768]{1,0:T(8,128)(2,1)} %wo.1, bf16[96,3072]{1,0:T(8,128)(2,1)} %wu.1, ...), custom_call_target="tpu_custom_call" | custom-call | tf_op jit(solution)/shard_map/gather_weights/pallas_call | solution.py:200
  240.0 4.1 convolution_convert_fusion.3
  244.2 2.9 fusion.37
  247.1 6.2 copy.57
  253.3 4.6 all-to-all-start
  262.2 3.2 sort.30.cloned.1.call-done
  267.7 48.9 %gather_fusion.1 = s32[6144]{0:T(1024)S(1)} fusion(s32[12,512]{1,0:T(8,128)S(1)} %bitcast.189, s32[6144]{0:T(1024)S(1)} %bitcast.190), kind=kCustom, calls=%fused_computation.1 | custom fusion | bytes 98304 | tf_op jit(solution)/shard_map/jit(take_along_axis)/gather | solution.py:516
  316.7 34.5 %all-to-all-done = bf16[12,192,512]{1,0,2:T(8,128)(2,1)} async-done(((bf16[12,192,512]{1,0,2:T(8,128)(2,1)}), bf16[12,192,512]{1,0,2:T(8,128)(2,1)}, u32[]{:S(2)}, u32[]{:S(2)}) %all-to-all-start) | async-done | bytes 2359328 | tf_op jit(solution)/shard_map/all_to_all | solution.py:623
  351.2 7.2 fusion.31
  358.3 4.2 reshape.478
  362.5 1.0 fusion.102
  363.6 3.1 fusion.25
  366.7 1.4 fusion.22
  368.1 2.7 fusion.56
  370.8 4.6 fusion.47
  375.4 3.7 copy.70
  379.2 4.3 reshape.559
  383.4 7.1 all-to-all-start.2
  391.7 1.2 slice.120
  393.6 18.4 %all-to-all-done.2 = bf16[32,2,6144]{2,1,0:T(2,128)(2,1)} async-done(((bf16[32,2,6144]{2,1,0:T(2,128)(2,1)}), bf16[32,2,6144]{2,1,0:T(2,128)(2,1)}, u32[]{:S(2)}, u32[]{:S(2)}) %all-to-all-start.2) | async-done | bytes 786464 | tf_op jit(solution)/shard_map/all_to_all | solution.py:632
  412.0 4.3 reshape.560
  416.3 4.4 fusion.48
  421.9 20.2 %multiply_convert_fusion = (bf16[512,3072]{1,0:T(8,128)(2,1)S(1)}, f32[512,3072]{1,0:T(8,128)}, f32[512,3072]{1,0:T(8,128)}) fusion(bf16[768,3072]{1,0:T(8,128)(2,1)} %bitcast.225, f32[512,768]{1,0:T(8,128)S(1)} %get-tuple-element.118, f32[768]{0:T(1024)S(1)} %add.170, f32[768]{0:T(1024)S(1)} %mul.228, f32[512]{0:T(512)S(1)} %add_rsqrt_fusion.1, ...), kind=kOutput, calls=%fused_computation.18 | convolution fusion | flops 2520121344 | bytes 22030336 | tf_op jit(solution)/shard_map/dot_general | solution.py:646
  442.3 2.8 fusion.105
  445.4 2.1 multiply_reduce_fusion.2
  448.1 8.9 %add_convert_fusion = bf16[512,3072]{1,0:T(8,128)(2,1)} fusion(f32[512,3072]{1,0:T(8,128)} %get-tuple-element.108, f32[512,3072]{1,0:T(8,128)} %get-tuple-element.119, bf16[3072,768]{1,0:T(8,128)(2,1)S(1)} %bitcast.232, f32[512,768]{1,0:T(8,128)S(1)} %get-tuple-element.121, f32[512]{0:T(512)S(1)} %get-tuple-element.126, ...), kind=kOutput, calls=%fused_computation.17 | convolution fusion | flops 2443051008 | bytes 22822912 | tf_op jit(solution)/shard_map/dot_general | solution.py:661
  456.9 5.4 multiply_reduce_fusion.3
  462.9 1.1 copy-done.2
  464.0 1.7 convolution_convert_fusion.5
  465.7 2.3 copy.72
  468.0 4.6 fusion.43
  472.6 3.8 copy.73
  476.4 4.7 reshape.561
  481.0 26.3 %all_to_all.25 = bf16[32,2,6144]{2,1,0:T(2,128)(2,1)} all-to-all(bf16[32,2,6144]{2,1,0:T(2,128)(2,1)} %reshape.561), channel_id=1, replica_groups=mesh['ctx'=32,'wsh'=8] {'ctx'}, dimensions={0} | all-to-all | bytes 1572864 | tf_op jit(solution)/shard_map/all_to_all | solution.py:679
  507.3 4.3 reshape.562
  511.6 4.3 fusion.53
  515.9 3.1 multiply_reduce_fusion
  519.1 1.6 multiply_convert_fusion.1
  521.9 1.2 fusion.59
  523.0 1.8 fusion.57
  525.6 3.1 fusion.38
  528.7 6.1 copy.83
  534.8 4.8 all-to-all-start.4
  540.6 2.9 convolution_convert_fusion.4
  543.5 6.8 convolution_convert_fusion.1
  550.4 5.4 convolution_convert_fusion
  555.8 77.2 %all-to-all-done.4 = bf16[12,192,512]{1,0,2:T(8,128)(2,1)} async-done(((bf16[12,192,512]{1,0,2:T(8,128)(2,1)}), bf16[12,192,512]{1,0,2:T(8,128)(2,1)}, u32[]{:S(2)}, u32[]{:S(2)}) %all-to-all-start.4) | async-done | bytes 2359328 | tf_op jit(solution)/shard_map/all_to_all | solution.py:685
  633.0 5.7 fusion.34
  639.9 3.9 convolution_convert_fusion.2
  643.7 3.2 add_bitcast_fusion
  646.9 152.0 %reduce_grads.1 = (bf16[96,1152]{1,0:T(8,128)(2,1)}, bf16[96,384]{1,0:T(8,128)(2,1)}, bf16[96,1536]{1,0:T(8,128)(2,1)}, bf16[384,384]{1,0:T(8,128)(2,1)}, f32[8,768]{1,0:T(8,128)}) custom-call(bf16[2,4,96,2304]{3,2,1,0:T(8,128)(2,1)} %bitcast.196, bf16[2,4,96,768]{3,2,1,0:T(8,128)(2,1)} %bitcast.193, bf16[2,4,96,3072]{3,2,1,0:T(8,128)(2,1)} %bitcast.194, ...), custom_call_target="tpu_custom_call" | custom-call | tf_op jit(solution)/shard_map/reduce_grads/pallas_call | solution.py:448
  798.9 1.0 dynamic-slice_convert_fusion
  803.8 1.2 slice.121
  805.0 1.3 constant_dynamic-slice_fusion
  807.7 1.5 dynamic-slice_convert_fusion.1
  (155 shorter events, 22.6 us)
Async XLA Ops:
  7.2 17.3 %copy-start.22 = (s32[2]{0:T(128)S(1)}, s32[2]{0:T(128)}, u32[]{:S(2)}) copy-start(s32[2]{0:T(128)} %constant.279) | copy-start | bytes 28
  7.2 17.4 %copy-start.21 = (s32[2]{0:T(128)S(1)}, s32[2]{0:T(128)}, u32[]{:S(2)}) copy-start(s32[2]{0:T(128)} %constant.282) | copy-start | bytes 28
  7.2 17.1 %copy-start.15 = (s32[1,12,512]{2,0,1:T(1,128)S(1)}, s32[1,12,512]{2,0,1:T(1,128)}, u32[]{:S(2)}) copy-start(s32[1,12,512]{2,0,1:T(1,128)} %param.18) | copy-start | bytes 73732
  7.2 40.7 %copy-start.19 = (s32[1,512]{1,0:T(1,128)S(1)}, s32[1,512]{1,0:T(1,128)}, u32[]{:S(2)}) copy-start(s32[1,512]{1,0:T(1,128)} %param.19) | copy-start | bytes 6148
  115.4 17.3 %copy-start.18 = (s32[1,512]{1,0:T(1,128)S(1)}, s32[1,512]{1,0:T(1,128)}, u32[]{:S(2)}) copy-start(s32[1,512]{1,0:T(1,128)} %param.20) | copy-start | bytes 6148
  115.4 17.9 %copy-start.20 = (bf16[4,96]{1,0:T(4,128)(2,1)S(1)}, bf16[4,96]{1,0:T(4,128)(2,1)}, u32[]{:S(2)}) copy-start(bf16[4,96]{1,0:T(4,128)(2,1)} %param.25) | copy-start | bytes 2308
  115.4 124.5 %copy-start.25 = (bf16[1,512,768]{2,1,0:T(8,128)(2,1)S(1)}, bf16[1,512,768]{2,1,0:T(8,128)(2,1)}, u32[]{:S(2)}) copy-start(bf16[1,512,768]{2,1,0:T(8,128)(2,1)} %param.16) | copy-start | bytes 2359300
  122.2 131.1 %all-to-all-start.1 = ((s32[32,1,384]{2,1,0:T(1,128)}), s32[32,1,384]{2,1,0:T(1,128)S(1)}, u32[]{:S(2)}, u32[]{:S(2)}) async-start(s32[32,1,384]{2,1,0:T(1,128)} %reshape.557), calls=%async_computation.1 | async-start | bytes 98304 | tf_op jit(solution)/shard_map/all_to_all | solution.py:624
  253.3 97.9 %all-to-all-start = ((bf16[12,192,512]{1,0,2:T(8,128)(2,1)}), bf16[12,192,512]{1,0,2:T(8,128)(2,1)}, u32[]{:S(2)}, u32[]{:S(2)}) async-start(bf16[12,192,512]{1,0,2:T(8,128)(2,1)} %copy.57), calls=%async_computation | async-start | bytes 8388608 | tf_op jit(solution)/shard_map/all_to_all | solution.py:623
  257.9 7.6 sort.30.cloned.1.call-start
  261.9 109.0 %sort.32.cloned.1.call-start = ((), (), s32[]{:S(2)}) async-start(), calls=%async_computation.6 | async-start | bytes 196640 | tf_op jit(solution)/shard_map/jit(argsort)/sort | solution.py:523
  267.7 83.5 %copy-start.16 = (s32[12,512]{1,0:T(8,128)S(1)}, s32[12,512]{1,0:T(8,128)}, u32[]{:S(2)}) copy-start(s32[12,512]{1,0:T(8,128)} %get-tuple-element.58) | copy-start | bytes 73732
  363.5 4.5 copy-start.6
  363.6 4.5 copy-start.8
  363.6 4.6 copy-start.11
  383.4 28.6 %all-to-all-start.2 = ((bf16[32,2,6144]{2,1,0:T(2,128)(2,1)}), bf16[32,2,6144]{2,1,0:T(2,128)(2,1)}, u32[]{:S(2)}, u32[]{:S(2)}) async-start(bf16[32,2,6144]{2,1,0:T(2,128)(2,1)} %reshape.559), calls=%async_computation.2 | async-start | bytes 1572864 | tf_op jit(solution)/shard_map/all_to_all | solution.py:632
  416.3 4.4 copy-start.24
  416.3 4.4 copy-start.26
  420.7 21.5 %copy-start.10 = (bf16[12,64,512]{2,1,0:T(8,128)(2,1)}, bf16[12,64,512]{2,1,0:T(8,128)(2,1)S(1)}, u32[]{:S(2)}) copy-start(bf16[12,64,512]{2,1,0:T(8,128)(2,1)S(1)} %fusion.48) | copy-start | bytes 2359300
  420.7 21.5 %slice-start.2 = ((s8[4718592]{0:T(1024)(128)(4,1)}), s8[4194304]{0:T(1024)(128)(4,1)S(1)}, s32[]{:S(2)}) async-start(s8[4718592]{0:T(1024)(128)(4,1)} %bitcast.229), calls=%async_computation.11 | async-start | bytes 8388608
  421.6 40.8 %copy-start.4 = (f32[512,768]{1,0:T(8,128)}, f32[512,768]{1,0:T(8,128)S(1)}, u32[]{:S(2)}) copy-start(f32[512,768]{1,0:T(8,128)S(1)} %get-tuple-element.118) | copy-start | bytes 4718596
  421.9 20.3 %slice-start.3 = ((s8[4718592]{0:T(1024)(128)(4,1)}), s8[524288]{0:T(1024)(128)(4,1)S(1)}, s32[]{:S(2)}) async-start(s8[4718592]{0:T(1024)(128)(4,1)} %bitcast.229), calls=%async_computation.12 | async-start | bytes 1048576
  442.2 2.8 copy-start.29
  442.3 3.1 copy-start.13
  445.0 11.9 %copy-start = (f32[512,768]{1,0:T(8,128)}, f32[512,768]{1,0:T(8,128)S(1)}, u32[]{:S(2)}) copy-start(f32[512,768]{1,0:T(8,128)S(1)} %get-tuple-element.121) | copy-start | bytes 4718596
  445.1 11.9 %slice-start = ((s8[4718592]{0:T(1024)(128)(4,1)}), s8[4194304]{0:T(1024)(128)(4,1)S(1)}, s32[]{:S(2)}) async-start(s8[4718592]{0:T(1024)(128)(4,1)} %bitcast.226), calls=%async_computation.9 | async-start | bytes 8388608
  448.1 8.9 %slice-start.1 = ((s8[4718592]{0:T(1024)(128)(4,1)}), s8[524288]{0:T(1024)(128)(4,1)S(1)}, s32[]{:S(2)}) async-start(s8[4718592]{0:T(1024)(128)(4,1)} %bitcast.226), calls=%async_computation.10 | async-start | bytes 1048576
  462.8 1.1 copy-start.2
  511.6 4.4 copy-start.12
  519.1 1.7 copy-start.9
  520.7 1.1 copy-start.7
  524.9 0.8 copy-start.28
  534.8 5.8 copy-start.3
  534.8 98.1 %all-to-all-start.4 = ((bf16[12,192,512]{1,0,2:T(8,128)(2,1)}), bf16[12,192,512]{1,0,2:T(8,128)(2,1)}, u32[]{:S(2)}, u32[]{:S(2)}) async-start(bf16[12,192,512]{1,0,2:T(8,128)(2,1)} %copy.83), calls=%async_computation.4 | async-start | bytes 8388608 | tf_op jit(solution)/shard_map/all_to_all | solution.py:685
  539.7 3.9 copy-start.5
  540.6 9.8 %copy-start.17 = (f32[8,768]{1,0:T(8,128)}, f32[8,768]{1,0:T(8,128)S(1)}, u32[]{:S(2)}) copy-start(f32[8,768]{1,0:T(8,128)S(1)} %scatter.25.refs_4_) | copy-start | bytes 73732
  543.5 6.9 copy-start.1
  543.5 6.9 copy-start.14
  543.5 6.9 copy-start.30
  638.7 1.1 copy-start.27
  639.9 3.9 copy-start.23
Sparse Core Ops, SparseCore 0:
  262.0 3.2 sort.34.cloned.1.call-done
  268.6 3.4 sort.36.cloned.1.call-done
  (2 shorter events, 0.0 us)
